TPU v7x, 32 devices: a whole 2x2x4 slice. The times are simulated.
32 devices in a mesh: table: 16 (over z, y, core), rep: 2 (over x).
Axes of the slice: x: 2, y: 2, z: 4, core: 2. Of those that a mesh axis runs over, the one named last changes fastest.
Arguments:
- bag_rows: int32 [32, 1024, 8], P(('table', 'rep')), may hold values from 0 to 2047
- bag_owner: int32 [32, 1024, 8], P(('table', 'rep')), may hold values from 0 to 15, all different within a row; in each aligned block of 1024 rows (0 to 1023, 1024 to 2047, ..., all dimensions but the last counted through in order) at most 768 rows name the same one
- bag_weight: float32 [32, 1024, 8], P(('table', 'rep')), may hold values from 0.25 to 2
- tables: bfloat16 [4, 32768, 128], P(None, 'table'), may hold values from -3 to 3
- returning: int32 [32], P(('table', 'rep')), may hold values 0 or 1
- home: int32 [32], P(('table', 'rep')), may hold values from 0 to 1
- entry: int32 [32], P(('table', 'rep')), may hold values from 0 to 7
- stores: bfloat16 [256, 30, 512], P(('table', 'rep')), may hold values from -6 to 6
- conv_weight: bfloat16 [4, 1536, 512], P(None, 'table'), may hold values from -0.15625 to 0.15625
- norm_gain: float32 [4, 512], replicated, may hold values from 0.1 to 1.9
Outputs:
- hidden: bfloat16 [32, 1024, 512], P(('table', 'rep'))
Inputs may be any that keep to these rules, and one draw needn't show every extreme that they name: `bag_owner`: the 8 ids of one slot name different owners. Among the slots of one device no owner is named by more than 768 ids, and in some devices' slots one owner is named by exactly 768.
All inputs are finite; a program needn't handle non-finite values. No bound on the sum of `returning` on one device may be relied on, other than what follows from the above.
Results may differ from a plain program's by a relative error of at most 0.0057.
Values may be sent and summed in bfloat16 or wider, within the bound.
No kernel may reach another device: no remote copies, remote signals or barrier semaphores. Data moves between devices by JAX's collectives and lax.ppermute only.
A program may use at most 64 MiB of HBM per device.

v0:
```python
import functools
import jax
import jax.numpy as jnp
from jax import lax
from jax.experimental import pallas as pl
from jax.experimental.pallas import tpu as pltpu
from jax.sharding import PartitionSpec as P

table_of_id = (0, 1, 2, 2, 3, 3, 3, 3)
bag_bounds = ((0, 1), (1, 2), (2, 4), (4, 8))
epsilon = 1e-05
part_ends = (0.25, 2 / 3, 1.0)
stage_parts = (2, 3)
megabyte = 1024 * 1024


def prep_kernel(cuts, shard_rows, rows_ref, owner_ref, request_ref, place_ref):
    owner = owner_ref[...]
    rows = rows_ref[...]
    owners = request_ref.shape[0]
    width, slots = owner.shape
    value_bits = (len(bag_bounds) * shard_rows).bit_length()
    owner_ids = lax.broadcasted_iota(jnp.int32, (owners, slots), 0)
    lane = lax.broadcasted_iota(jnp.int32, (owners, slots), 1)
    value = jnp.zeros((owners, slots), jnp.int32)
    for k in range(width):
        named = owner[k : k + 1, :] == owner_ids
        value = jnp.where(named, rows[k : k + 1, :] + (table_of_id[k] * shard_rows + 1), value)
    present = jnp.where(value > 0, 1, 0)
    rank = present
    step = 1
    while step < slots:
        rank = rank + jnp.where(lane >= step, pltpu.roll(rank, step, 1), 0)
        step *= 2
    rank = rank - present
    place = jnp.zeros((width, slots), jnp.int32)
    for number in range(owners):
        place = jnp.where(owner == number, rank[number : number + 1, :], place)
    landing = jnp.zeros((width, slots), jnp.int32)
    for start, stop in zip(cuts[:-1], cuts[1:]):
        where = owners * start + owner * (stop - start) + place - start
        landing = jnp.where(place >= start, where, landing)
    place_ref[...] = landing
    packed = jnp.where(value > 0, ((lane - rank) << value_bits) + value, 0)
    step = 1
    level = value_bits
    while step < slots:
        moving = jnp.where(((packed >> level) & 1) == 1, packed, 0)
        packed = (packed - moving) + pltpu.roll(moving, slots - step, 1)
        step *= 2
        level += 1
    value = jnp.maximum((packed & ((1 << value_bits) - 1)) - 1, 0)
    for number in range(owners):
        request_ref[number] = value[number : number + 1, : request_ref.shape[2]]


def pass_kernel(*refs):
    pass


def tie(array, *others):
    anywhere = pl.BlockSpec(memory_space=pl.ANY)
    return pl.pallas_call(
        pass_kernel,
        out_shape=jax.ShapeDtypeStruct(array.shape, array.dtype),
        in_specs=[anywhere] * (1 + len(others)),
        out_specs=anywhere,
        input_output_aliases={0: 0},
        name="tie",
    )(array, *others)


def gather_kernel(capacity, first, index_ref, table_ref, *refs):
    out_ref, narrow, wide, picked, packed, index, index_sem, table_sems, out_sems = refs[-9:]
    owners, piece, _ = out_ref.shape
    unroll = 32 if piece % 32 == 0 else 16
    blocks = table_sems.shape[0]
    block_rows = table_ref.shape[0] // blocks
    table_copies = []
    for block in range(blocks):
        part = pl.ds(block * block_rows, block_rows)
        copy = pltpu.make_async_copy(table_ref.at[part, :], narrow.at[part, :], table_sems.at[block])
        copy.start()
        table_copies.append(copy)
    index_copy = pltpu.make_async_copy(index_ref, index, index_sem)
    index_copy.start()
    rows = 256

    for block in range(blocks):
        table_copies[block].wait()

        def widen(step, carry, block=block):
            base = pl.multiple_of(block * block_rows + step * rows, rows)
            wide[pl.ds(base, rows), :] = narrow[pl.ds(base, rows), :].astype(jnp.float32)
            return carry

        lax.fori_loop(0, block_rows // rows, widen, 0)
    index_copy.wait()
    copies = []
    for number in range(owners):
        origin = number * capacity + first

        def some_rows(block, carry, origin=origin):
            base = pl.multiple_of(block * unroll, unroll)
            picks = [index[origin + base + i] for i in range(unroll)]
            found = [wide[pl.ds(pick, 1), :] for pick in picks]
            for i in range(unroll):
                picked[pl.ds(base + i, 1), :] = found[i]
            return carry

        lax.fori_loop(0, piece // unroll, some_rows, 0)
        packed[number] = picked[...].astype(jnp.bfloat16)
        copy = pltpu.make_async_copy(packed.at[number], out_ref.at[number], out_sems.at[number])
        copy.start()
        copies.append(copy)
    for copy in copies:
        copy.wait()


def stage_kernel(
    pieces, sources, first, aliased, place_ref, me_ref, weight_ref, carried_ref, gain_ref, *refs
):
    piece_refs = refs[:pieces]
    filter_refs = refs[pieces : pieces + sources]
    refs = refs[pieces + sources + aliased :]
    out_ref, state_ref, table, picked, filters, first_buf, second_buf, result = refs[:8]
    filter_sems, out_sems = refs[8:]
    width, slots, lanes = picked.shape
    layers = filters.shape[0]
    filter_copies = []
    if sources == 1:
        filter_copies.append(pltpu.make_async_copy(filter_refs[0], filters, filter_sems.at[0]))
    else:
        held, half, depth, _ = filter_refs[0].shape
        for group, filter_ref in enumerate(filter_refs):
            bits, base = block_place(group, me_ref[1])
            for number in range(held):
                owner = me_ref[0] ^ (4 * number + bits)
                rows = pl.ds(pl.multiple_of(owner * depth, depth), depth)
                layer = pl.ds(base * (half // 2), filter_ref.shape[1])
                filter_copies.append(
                    pltpu.make_async_copy(
                        filter_ref.at[number],
                        filters.at[layer, rows, :],
                        filter_sems.at[group * held + number],
                    )
                )
    for copy in filter_copies:
        copy.start()
    start = 0
    for piece_ref in piece_refs:
        count = piece_ref.shape[0]
        rows = 256

        def widen(step, carry, piece_ref=piece_ref, start=start):
            base = pl.multiple_of(step * rows, rows)
            table[pl.ds(start + base, rows), :] = piece_ref[pl.ds(base, rows), :].astype(jnp.float32)
            return carry

        lax.fori_loop(0, count // rows, widen, 0)
        start += count

    def some_slots(step, carry):
        base = pl.multiple_of(step * 8, 8)
        for k in range(width):
            picks = [place_ref[k, first + base + i] for i in range(8)]
            rows = [table[pl.ds(pick, 1), :] for pick in picks]
            for i in range(8):
                picked[k, pl.ds(base + i, 1), :] = rows[i]
        return carry

    lax.fori_loop(0, slots // 8, some_slots, 0)
    front = 16
    weights = jnp.transpose(weight_ref[:, first : first + slots])
    for t, (lower, upper) in enumerate(bag_bounds):
        total = picked[lower] * weights[:, lower : lower + 1]
        for k in range(lower + 1, upper):
            total = total + picked[k] * weights[:, k : k + 1]
        total = total.astype(jnp.bfloat16).astype(jnp.float32)
        first_buf[front:, t * lanes : (t + 1) * lanes] = total

    for copy in filter_copies:
        copy.wait()
    offset = 0
    out_copies = []
    for layer in range(layers):
        dilation = 2**layer
        span = 2 * dilation
        source, target = (first_buf, second_buf) if layer % 2 == 0 else (second_buf, first_buf)
        source[front - span : front, :] = carried_ref[offset : offset + span, :]
        state_ref[offset : offset + span, :] = source[front + slots - span : front + slots, :]
        offset += span
        for begin in range(0, slots, 256):
            rows = min(256, slots - begin)
            base = front + begin
            taps = [
                source[base - tap * dilation : base - tap * dilation + rows, :].astype(jnp.bfloat16)
                for tap in range(3)
            ]
            output = jnp.dot(
                jnp.concatenate(taps, axis=1), filters[layer], preferred_element_type=jnp.float32
            )
            mean = jnp.mean(output, axis=-1, keepdims=True)
            centred = output - mean
            spread = jnp.mean(centred * centred, axis=-1, keepdims=True)
            active = jnp.maximum(
                centred * lax.rsqrt(spread + epsilon) * gain_ref[layer : layer + 1, :], 0.0
            )
            if layer % 2 == 1:
                active = active + target[base : base + rows, :]
            active = active.astype(jnp.bfloat16)
            if layer == layers - 1:
                result[begin : begin + rows, :] = active
                copy = pltpu.make_async_copy(
                    result.at[pl.ds(begin, rows), :],
                    out_ref.at[pl.ds(first + begin, rows), :],
                    out_sems.at[len(out_copies)],
                )
                copy.start()
                out_copies.append(copy)
            else:
                target[base : base + rows, :] = active.astype(jnp.float32)
    for copy in out_copies:
        copy.wait()


def swapped(array, axis, distance):
    pairs = [(source, source ^ distance) for source in range(lax.axis_size(axis))]
    return lax.ppermute(array, axis, pairs)


def block_place(number, side):
    kind = number % 5
    bits = (2 if kind in (1, 3, 4) else 0) + number // 5
    base = 2 * (side if kind < 2 else 1 - side) + (1 if kind == 4 else 0)
    return bits, base


def ordered_filters(blocks, me):
    count = blocks[0].shape[0]
    owners = 4 * count
    quarter = blocks[0].shape[1] // 2
    layers = 4 * quarter
    whole = jnp.zeros((owners, layers) + blocks[0].shape[2:], blocks[0].dtype)
    for number, block in enumerate(blocks):
        bits, base = block_place(number, me[1])
        for shard in range(count):
            owner = me[0] ^ (4 * shard + bits)
            whole = lax.dynamic_update_slice(
                whole, block[shard][None], (owner, base * quarter, 0, 0)
            )
    return whole.transpose(1, 0, 2, 3).reshape(layers, -1, whole.shape[-1])


def carried_rows(returning, home, entry, stores):
    copies = lax.axis_size("rep")
    me = lax.axis_index("rep")
    by_position = stores.transpose(1, 0, 2)
    positions, _, channels = by_position.shape
    carried = jnp.zeros((positions, channels), stores.dtype)
    for shift in range(copies):
        arrived = by_position
        if shift:
            pairs = [(source, (source + shift) % copies) for source in range(copies)]
            arrived = lax.ppermute(by_position, "rep", pairs)
        wanted = (returning[0] > 0) & (home[0] == (me + copies - shift) % copies)
        chosen = lax.dynamic_index_in_dim(arrived, entry[0], 1, keepdims=False)
        carried = jnp.where(wanted, chosen, carried)
    return carried.astype(jnp.float32)


def local(
    bag_rows, bag_owner, bag_weight, tables, returning, home, entry, stores, conv_weight, norm_gain
):
    owners = lax.axis_size("table")
    samples_here, slot_count, bag_width = bag_rows.shape
    token_count = samples_here * slot_count
    shard_rows = tables.shape[1]
    row_width = tables.shape[2]
    channels = conv_weight.shape[-1]
    capacity = min(token_count, (3 * token_count * bag_width + 2 * owners - 1) // (2 * owners))
    cuts = [0] + [round(capacity * end) // 16 * 16 for end in part_ends]
    slot_cuts = [0] + [cuts[part] for part in stage_parts[:-1]] + [token_count]
    smem = pl.BlockSpec(memory_space=pltpu.SMEM)
    vmem = pl.BlockSpec(memory_space=pltpu.VMEM)
    anywhere = pl.BlockSpec(memory_space=pl.ANY)

    me = jnp.stack([lax.axis_index("table"), lax.axis_index("rep") % 2]).astype(jnp.int32)
    half = conv_weight.shape[0] // 2
    shard = lax.dynamic_slice_in_dim(conv_weight, me[1] * half, half, 0)
    middle = owners // 8
    line = [shard] + [swapped(shard, "table", 4 * step) for step in range(1, middle + 1)]
    state = carried_rows(returning, home, entry, stores)
    rows_by_slot = bag_rows.reshape(token_count, bag_width).T
    owner_by_slot = bag_owner.reshape(token_count, bag_width).T
    requests, place = pl.pallas_call(
        functools.partial(prep_kernel, cuts, shard_rows),
        out_shape=(
            jax.ShapeDtypeStruct((owners, 1, capacity), jnp.int32),
            jax.ShapeDtypeStruct((bag_width, token_count), jnp.int32),
        ),
        in_specs=[vmem, vmem],
        out_specs=(vmem, vmem),
        compiler_params=pltpu.CompilerParams(vmem_limit_bytes=8 * megabyte),
        name="prep",
    )(rows_by_slot, owner_by_slot)
    received = lax.all_to_all(requests, "table", split_axis=0, concat_axis=0, tiled=True)
    received = received.reshape(owners * capacity)
    flat_table = tables.reshape(-1, row_width)
    returned = []
    sent = []
    for number in range(len(part_ends)):
        piece = cuts[number + 1] - cuts[number]
        if number == 1:
            line = line + [swapped(line[middle], "table", 4 * step) for step in range(1, middle)]
            sent[0] = tie(sent[0], *line[middle + 1 :])
        earlier = sent[-1:] if sent else line[1:]
        sent.append(
            pl.pallas_call(
                functools.partial(gather_kernel, capacity, cuts[number]),
                out_shape=jax.ShapeDtypeStruct((owners, piece, row_width), jnp.bfloat16),
                in_specs=[anywhere] * (2 + len(earlier)),
                out_specs=anywhere,
                scratch_shapes=[
                    pltpu.VMEM(flat_table.shape, jnp.bfloat16),
                    pltpu.VMEM(flat_table.shape, jnp.float32),
                    pltpu.VMEM((piece, row_width), jnp.float32),
                    pltpu.VMEM((owners, piece, row_width), jnp.bfloat16),
                    pltpu.SMEM((owners * capacity,), jnp.int32),
                    pltpu.SemaphoreType.DMA,
                    pltpu.SemaphoreType.DMA((8,)),
                    pltpu.SemaphoreType.DMA((owners,)),
                ],
                compiler_params=pltpu.CompilerParams(vmem_limit_bytes=58 * megabyte),
                cost_estimate=pl.CostEstimate(
                    flops=0, bytes_accessed=20 * megabyte, transcendentals=0
                ),
                name="owner_gather",
            )(received, flat_table, *earlier)
        )
    line = tie(jnp.stack(line), sent[0])
    by_table = swapped(line, "table", 2)
    by_rep = swapped(line, "rep", 1)
    corner_low = swapped(by_rep[:, : half // 2], "table", 2)
    corner_high = swapped(by_table[:, half // 2 :], "rep", 1)
    near = [swapped(block, "table", 1) for block in (line, by_table, by_rep)]
    gates = [[], [sent[2], by_table, by_rep], [state, corner_low, corner_high] + near]
    for rows, gate in zip(sent, gates):
        if returned:
            rows = tie(rows, returned[-1], *gate)
        arrived = lax.all_to_all(rows, "table", split_axis=0, concat_axis=0, tiled=True)
        returned.append(arrived.reshape(-1, row_width))
    near = near + [swapped(block, "table", 1) for block in (corner_low, corner_high)]
    filters = [line, by_table, by_rep, corner_low, corner_high] + near
    if conv_weight.shape[1] % 16:
        filters = [ordered_filters(filters, me)]
    weight_by_slot = bag_weight.reshape(token_count, bag_width).T
    hidden = None
    for number, part in enumerate(stage_parts):
        first, last = slot_cuts[number], slot_cuts[number + 1]
        slots = last - first
        known = [] if hidden is None else [hidden]
        pieces = returned[:part]
        hidden, state = pl.pallas_call(
            functools.partial(stage_kernel, part, len(filters), first, len(known)),
            out_shape=(
                jax.ShapeDtypeStruct((token_count, channels), jnp.bfloat16),
                jax.ShapeDtypeStruct(state.shape, jnp.float32),
            ),
            in_specs=[smem] * 2
            + [vmem] * (3 + part)
            + [anywhere] * (len(filters) + len(known)),
            out_specs=(anywhere, vmem),
            scratch_shapes=[
                pltpu.VMEM((owners * cuts[part], row_width), jnp.float32),
                pltpu.VMEM((bag_width, slots, row_width), jnp.float32),
                pltpu.VMEM((conv_weight.shape[0], 3 * channels, channels), jnp.bfloat16),
                pltpu.VMEM((slots + 16, channels), jnp.float32),
                pltpu.VMEM((slots + 16, channels), jnp.float32),
                pltpu.VMEM((slots, channels), jnp.bfloat16),
                pltpu.SemaphoreType.DMA((10 * (owners // 4),)),
                pltpu.SemaphoreType.DMA(((slots + 255) // 256,)),
            ],
            input_output_aliases={5 + part + len(filters): 0} if known else {},
            compiler_params=pltpu.CompilerParams(vmem_limit_bytes=56 * megabyte),
            cost_estimate=pl.CostEstimate(
                flops=2 * slots * 3 * channels * channels * conv_weight.shape[0],
                bytes_accessed=24 * megabyte,
                transcendentals=0,
            ),
            name="stage",
        )(place, me, weight_by_slot, state, norm_gain, *pieces, *filters, *known)
    return hidden.reshape(samples_here, slot_count, channels)


def solution(mesh):
    in_specs = (
        P(("table", "rep"), None, None),
        P(("table", "rep"), None, None),
        P(("table", "rep"), None, None),
        P(None, "table", None),
        P(("table", "rep")),
        P(("table", "rep")),
        P(("table", "rep")),
        P(("table", "rep"), None, None),
        P(None, "table", None),
        P(),
    )
    out_specs = P(("table", "rep"), None, None)
    return jax.shard_map(local, mesh=mesh, in_specs=in_specs, out_specs=out_specs, check_vma=False)
```

profile of v0, /device:TPU:0, one launch (start us, length us, event | category | flops | bytes accessed | tf_op | source)
XLA Modules:
  0.0 149.7 jit_solution(7197104570778051144)
XLA Ops:
  0.0 1.0 copy-done
  1.0 4.1 %collective-permute-start.2 = (bf16[2,96,512]{2,1,0:T(8,128)(2,1)S(1)}, bf16[2,96,512]{2,1,0:T(8,128)(2,1)S(1)}, u32[]{:S(2)}, u32[]{:S(2)}) collective-permute-start(bf16[2,96,512]{2,1,0:T(8,128)(2,1)S(1)} %constant_dynamic-slice_fusion), channel_id=1, source_target_pairs={{0,16},{2,18},{4,20},{6,22},{8,24},{10,26},{12,28},{14,30},{16,0},... | collective-permute-start | bytes 589832 | tf_op jit(solution)/shard_map/ppermute | solution.py:229
  5.1 1.6 %collective-permute-start.1 = (bf16[2,96,512]{2,1,0:T(8,128)(2,1)S(1)}, bf16[2,96,512]{2,1,0:T(8,128)(2,1)S(1)}, u32[]{:S(2)}, u32[]{:S(2)}) collective-permute-start(bf16[2,96,512]{2,1,0:T(8,128)(2,1)S(1)} %constant_dynamic-slice_fusion), channel_id=1, source_target_pairs={{0,8},{2,10},{4,12},{6,14},{8,0},{10,2},{12,4},{14,6},{16,24},{18,... | collective-permute-start | bytes 589832 | tf_op jit(solution)/shard_map/ppermute | solution.py:229
  6.7 7.6 %collective-permute-done.2.refs_1_ = bf16[2,96,512]{2,1,0:T(8,128)(2,1)S(1)} collective-permute-done((bf16[2,96,512]{2,1,0:T(8,128)(2,1)S(1)}, bf16[2,96,512]{2,1,0:T(8,128)(2,1)S(1)}, u32[]{:S(2)}, u32[]{:S(2)}) %collective-permute-start.2) | collective-permute-done | bytes 196640 | tf_op jit(solution)/shard_map/ppermute | solution.py:229
  14.3 0.6 collective-permute-start.3
  15.0 0.8 copy-done.1
  15.7 0.8 copy-done.2
  16.5 1.2 prep.1
  17.7 12.4 %all_to_all.20 = s32[16,1,768]{2,1,0:T(1,128)} all-to-all(s32[16,1,768]{2,1,0:T(1,128)S(1)} %get-tuple-element.11), channel_id=1, replica_groups=mesh['table'=16,'rep'=2] {'table'}, dimensions={0} | all-to-all | bytes 98304 | tf_op jit(solution)/shard_map/all_to_all | solution.py:307
  30.1 0.7 copy-done.14
  30.8 5.4 %owner_gather.3.refs_0_ = bf16[16,192,128]{2,1,0:T(8,128)(2,1)} custom-call(s32[12288]{0:T(1024)} %bitcast.51, bf16[8192,128]{1,0:T(8,128)(2,1)} %bitcast.41, bf16[2,96,512]{2,1,0:T(8,128)(2,1)} %copy-done.14, bf16[2,96,512]{2,1,0:T(8,128)(2,1)} %copy-done.12), custom_call_target="tpu_custom_call" | custom-call | bytes 20971520 | tf_op jit(solution)/shard_map/owner_gather/pallas_call | solution.py:319
  36.2 0.7 copy-done.16
  36.9 3.7 %all-to-all-start.1 = ((bf16[16,192,128]{2,1,0:T(8,128)(2,1)}), bf16[16,192,128]{2,1,0:T(8,128)(2,1)S(1)}, u32[]{:S(2)}, u32[]{:S(2)}) async-start(bf16[16,192,128]{2,1,0:T(8,128)(2,1)} %tie.4.refs_0_.refs_1_), calls=%async_computation.1 | async-start | bytes 1572864 | tf_op jit(solution)/shard_map/all_to_all | solution.py:351
  40.7 1.0 pad_maximum_fusion.refs_0_
  41.8 1.5 collective-permute-start.5
  43.3 1.8 %collective-permute-start.4 = (bf16[4,2,96,512]{3,2,1,0:T(8,128)(2,1)}, bf16[4,2,96,512]{3,2,1,0:T(8,128)(2,1)S(1)}, u32[]{:S(2)}, u32[]{:S(2)}) collective-permute-start(bf16[4,2,96,512]{3,2,1,0:T(8,128)(2,1)} %tie.5.refs_2_.refs_3_), channel_id=1, source_target_pairs={{0,4},{2,6},{4,0},{6,2},{8,12},{10,14},{12,8},{14,10},{16,20},{18,... | collective-permute-start | bytes 2359304 | tf_op jit(solution)/shard_map/ppermute | solution.py:229
  45.1 7.3 %owner_gather.4.refs_0_ = bf16[16,320,128]{2,1,0:T(8,128)(2,1)} custom-call(s32[12288]{0:T(1024)} %bitcast.52, bf16[8192,128]{1,0:T(8,128)(2,1)} %bitcast.42, bf16[16,192,128]{2,1,0:T(8,128)(2,1)} %tie.4.refs_0_.refs_1_), custom_call_target="tpu_custom_call" | custom-call | bytes 20971520 | tf_op jit(solution)/shard_map/owner_gather/pallas_call | solution.py:319
  52.4 6.4 %owner_gather.5.refs_2_.refs_0_ = bf16[16,256,128]{2,1,0:T(8,128)(2,1)} custom-call(s32[12288]{0:T(1024)} %bitcast.53, bf16[8192,128]{1,0:T(8,128)(2,1)} %bitcast.43, bf16[16,320,128]{2,1,0:T(8,128)(2,1)} %owner_gather.4.refs_0_), custom_call_target="tpu_custom_call" | custom-call | bytes 20971520 | tf_op jit(solution)/shard_map/owner_gather/pallas_call | solution.py:319
  58.8 2.9 %collective-permute-done.5.refs_4_.refs_5_ = bf16[4,2,96,512]{3,2,1,0:T(8,128)(2,1)S(1)} collective-permute-done((bf16[4,2,96,512]{3,2,1,0:T(8,128)(2,1)}, bf16[4,2,96,512]{3,2,1,0:T(8,128)(2,1)S(1)}, u32[]{:S(2)}, u32[]{:S(2)}) %collective-permute-start.5) | collective-permute-done | bytes 786464 | tf_op jit(solution)/shard_map/ppermute | solution.py:229
  61.7 7.3 %collective-permute-done.4.refs_3_.refs_4_ = bf16[4,2,96,512]{3,2,1,0:T(8,128)(2,1)S(1)} collective-permute-done((bf16[4,2,96,512]{3,2,1,0:T(8,128)(2,1)}, bf16[4,2,96,512]{3,2,1,0:T(8,128)(2,1)S(1)}, u32[]{:S(2)}, u32[]{:S(2)}) %collective-permute-start.4) | collective-permute-done | bytes 786464 | tf_op jit(solution)/shard_map/ppermute | solution.py:229
  69.0 0.9 copy-done.9
  69.8 0.3 copy-done.6
  70.1 4.9 %all-to-all-start.2 = ((bf16[16,320,128]{2,1,0:T(8,128)(2,1)}), bf16[16,320,128]{2,1,0:T(8,128)(2,1)S(1)}, u32[]{:S(2)}, u32[]{:S(2)}) async-start(bf16[16,320,128]{2,1,0:T(8,128)(2,1)} %tie.6), calls=%async_computation.2 | async-start | bytes 2621440 | tf_op jit(solution)/shard_map/all_to_all | solution.py:351
  75.0 0.5 collective-permute-start.8
  75.6 0.4 collective-permute-start.9
  76.0 1.0 copy.21
  77.0 1.6 %collective-permute-start = (bf16[30,8,512]{2,0,1:T(8,128)(2,1)S(1)}, bf16[30,8,512]{2,0,1:T(8,128)(2,1)S(1)}, u32[]{:S(2)}, u32[]{:S(2)}) collective-permute-start(bf16[30,8,512]{2,0,1:T(8,128)(2,1)S(1)} %bitcast.57), channel_id=1, source_target_pairs={{0,1},{1,0},{2,3},{3,2},{4,5},{5,4},{6,7},{7,6},{8,9},{9,8},{10,11... | collective-permute-start | bytes 737288 | tf_op jit(solution)/shard_map/ppermute | solution.py:265
  78.6 0.8 slice.8
  79.3 1.7 %collective-permute-start.6 = (bf16[4,1,96,512]{3,2,1,0:T(8,128)(2,1)}, bf16[4,1,96,512]{3,2,1,0:T(8,128)(2,1)}, u32[]{:S(2)}, u32[]{:S(2)}) collective-permute-start(bf16[4,1,96,512]{3,2,1,0:T(8,128)(2,1)} %slice.8), channel_id=1, source_target_pairs={{0,4},{2,6},{4,0},{6,2},{8,12},{10,14},{12,8},{14,10},{16,20},{18,... | collective-permute-start | bytes 1179656 | tf_op jit(solution)/shard_map/ppermute | solution.py:229
  81.0 0.8 slice.9
  81.8 3.6 %collective-permute-done = bf16[30,8,512]{2,0,1:T(8,128)(2,1)S(1)} collective-permute-done((bf16[30,8,512]{2,0,1:T(8,128)(2,1)S(1)}, bf16[30,8,512]{2,0,1:T(8,128)(2,1)S(1)}, u32[]{:S(2)}, u32[]{:S(2)}) %collective-permute-start) | collective-permute-done | bytes 245792 | tf_op jit(solution)/shard_map/ppermute | solution.py:265
  85.4 0.7 copy-done.18
  86.1 1.5 collective-permute-start.7
  89.5 1.4 fusion.carried_ref.refs_2_
  91.0 7.2 %collective-permute-done.6.refs_5_.refs_3_.refs_6_ = bf16[4,1,96,512]{3,2,1,0:T(8,128)(2,1)} collective-permute-done((bf16[4,1,96,512]{3,2,1,0:T(8,128)(2,1)}, bf16[4,1,96,512]{3,2,1,0:T(8,128)(2,1)}, u32[]{:S(2)}, u32[]{:S(2)}) %collective-permute-start.6) | collective-permute-done | bytes 393248 | tf_op jit(solution)/shard_map/ppermute | solution.py:229
  98.2 4.2 %all-to-all-done.2 = bf16[16,320,128]{2,1,0:T(8,128)(2,1)S(1)} async-done(((bf16[16,320,128]{2,1,0:T(8,128)(2,1)}), bf16[16,320,128]{2,1,0:T(8,128)(2,1)S(1)}, u32[]{:S(2)}, u32[]{:S(2)}) %all-to-all-start.2) | async-done | bytes 1310752 | tf_op jit(solution)/shard_map/all_to_all | solution.py:351
  102.4 1.1 copy-done.4
  103.5 8.1 %all-to-all-start.3 = ((bf16[16,256,128]{2,1,0:T(8,128)(2,1)}), bf16[16,256,128]{2,1,0:T(8,128)(2,1)S(1)}, u32[]{:S(2)}, u32[]{:S(2)}) async-start(bf16[16,256,128]{2,1,0:T(8,128)(2,1)} %tie.7), calls=%async_computation.3 | async-start | bytes 2097152 | tf_op jit(solution)/shard_map/all_to_all | solution.py:351
  111.6 0.5 collective-permute-start.11
  112.1 0.6 pad_add_fusion.me_ref
  112.7 0.9 collective-permute-done.11.refs_10_.refs_11_
  113.6 0.6 collective-permute-done.12.refs_11_.refs_12_
  114.2 0.2 copy-done.19
  114.4 0.6 copy-done.20
  114.9 13.5 %stage.2 = (bf16[1024,512]{1,0:T(8,128)(2,1)}, f32[30,512]{1,0:T(8,128)}) custom-call(s32[8,1024]{1,0:T(8,128)} %copy-done.3, s32[2]{0:T(128)} %pad_add_fusion.me_ref, f32[8,1024]{1,0:T(8,128)} %bitcast.58, f32[30,512]{1,0:T(8,128)} %fusion.carried_ref.refs_2_, f32[4,512]{1,0:T(4,128)} %gain_ref.3, bf16[3072,128]{1,0:T(8,128)(2,1)} %bitcast.48, ...), custom_call_target="tpu_custom_call" | custom-call | flops 3221225472 | bytes 25165824 | tf_op jit(solution)/shard_map/stage/pallas_call | solution.py:364
  128.5 6.0 %all-to-all-done.3 = bf16[16,256,128]{2,1,0:T(8,128)(2,1)S(1)} async-done(((bf16[16,256,128]{2,1,0:T(8,128)(2,1)}), bf16[16,256,128]{2,1,0:T(8,128)(2,1)S(1)}, u32[]{:S(2)}, u32[]{:S(2)}) %all-to-all-start.3) | async-done | bytes 1048608 | tf_op jit(solution)/shard_map/all_to_all | solution.py:351
  134.5 1.0 copy-done.11
  135.5 14.1 %stage.3 = (bf16[1024,512]{1,0:T(8,128)(2,1)}, f32[30,512]{1,0:T(8,128)}) custom-call(s32[8,1024]{1,0:T(8,128)} %copy-done.3, s32[2]{0:T(128)} %pad_add_fusion.me_ref, f32[8,1024]{1,0:T(8,128)} %bitcast.59, f32[30,512]{1,0:T(8,128)} %get-tuple-element.12.carried_ref, f32[4,512]{1,0:T(4,128)} %gain_ref.3, ...), custom_call_target="tpu_custom_call", output_to_operand_aliasing={{0}: (18, {})} | custom-call | flops 3221225472 | bytes 25165824 | tf_op jit(solution)/shard_map/stage/pallas_call | solution.py:364
  (45 shorter events, 0.3 us)
Async XLA Ops:
  0.0 1.0 copy-start
  1.0 13.3 %collective-permute-start.2 = (bf16[2,96,512]{2,1,0:T(8,128)(2,1)S(1)}, bf16[2,96,512]{2,1,0:T(8,128)(2,1)S(1)}, u32[]{:S(2)}, u32[]{:S(2)}) collective-permute-start(bf16[2,96,512]{2,1,0:T(8,128)(2,1)S(1)} %constant_dynamic-slice_fusion), channel_id=1, source_target_pairs={{0,16},{2,18},{4,20},{6,22},{8,24},{10,26},{12,28},{14,30},{16,0},... | collective-permute-start | bytes 589832 | tf_op jit(solution)/shard_map/ppermute | solution.py:229
  5.1 25.0 %collective-permute-start.1 = (bf16[2,96,512]{2,1,0:T(8,128)(2,1)S(1)}, bf16[2,96,512]{2,1,0:T(8,128)(2,1)S(1)}, u32[]{:S(2)}, u32[]{:S(2)}) collective-permute-start(bf16[2,96,512]{2,1,0:T(8,128)(2,1)S(1)} %constant_dynamic-slice_fusion), channel_id=1, source_target_pairs={{0,8},{2,10},{4,12},{6,14},{8,0},{10,2},{12,4},{14,6},{16,24},{18,... | collective-permute-start | bytes 589832 | tf_op jit(solution)/shard_map/ppermute | solution.py:229
  14.3 15.8 %copy-start.12 = (bf16[2,96,512]{2,1,0:T(8,128)(2,1)}, bf16[2,96,512]{2,1,0:T(8,128)(2,1)S(1)}, u32[]{:S(2)}) copy-start(bf16[2,96,512]{2,1,0:T(8,128)(2,1)S(1)} %collective-permute-done.2.refs_1_) | copy-start | bytes 589828
  14.3 21.9 %collective-permute-start.3 = (bf16[2,96,512]{2,1,0:T(8,128)(2,1)S(1)}, bf16[2,96,512]{2,1,0:T(8,128)(2,1)S(1)}, u32[]{:S(2)}, u32[]{:S(2)}) collective-permute-start(bf16[2,96,512]{2,1,0:T(8,128)(2,1)S(1)} %collective-permute-done.2.refs_1_), channel_id=1, source_target_pairs={{0,8},{2,10},{4,12},{6,14},{8,0},{10,2},{12,4},{14,6},{16,24},{18,... | collective-permute-start | bytes 589832 | tf_op jit(solution)/shard_map/ppermute | solution.py:229
  15.0 0.8 copy-start.1
  15.7 0.8 copy-start.2
  17.7 12.4 %copy-start.3 = (s32[8,1024]{1,0:T(8,128)}, s32[8,1024]{1,0:T(8,128)S(1)}, u32[]{:S(2)}) copy-start(s32[8,1024]{1,0:T(8,128)S(1)} %get-tuple-element.10.place_ref) | copy-start | bytes 98308
  30.1 0.7 copy-start.14
  36.2 0.7 copy-start.16
  36.9 3.8 %copy-start.13 = (bf16[2,96,512]{2,1,0:T(8,128)(2,1)S(1)}, bf16[2,96,512]{2,1,0:T(8,128)(2,1)}, u32[]{:S(2)}) copy-start(bf16[2,96,512]{2,1,0:T(8,128)(2,1)} %copy-done.12) | copy-start | bytes 589828
  36.9 3.8 %copy-start.15 = (bf16[2,96,512]{2,1,0:T(8,128)(2,1)S(1)}, bf16[2,96,512]{2,1,0:T(8,128)(2,1)}, u32[]{:S(2)}) copy-start(bf16[2,96,512]{2,1,0:T(8,128)(2,1)} %copy-done.14) | copy-start | bytes 589828
  36.9 3.8 %copy-start.17 = (bf16[2,96,512]{2,1,0:T(8,128)(2,1)S(1)}, bf16[2,96,512]{2,1,0:T(8,128)(2,1)}, u32[]{:S(2)}) copy-start(bf16[2,96,512]{2,1,0:T(8,128)(2,1)} %copy-done.16) | copy-start | bytes 589828
  36.9 32.1 %all-to-all-start.1 = ((bf16[16,192,128]{2,1,0:T(8,128)(2,1)}), bf16[16,192,128]{2,1,0:T(8,128)(2,1)S(1)}, u32[]{:S(2)}, u32[]{:S(2)}) async-start(bf16[16,192,128]{2,1,0:T(8,128)(2,1)} %tie.4.refs_0_.refs_1_), calls=%async_computation.1 | async-start | bytes 1572864 | tf_op jit(solution)/shard_map/all_to_all | solution.py:351
  41.8 19.9 %collective-permute-start.5 = (bf16[4,2,96,512]{3,2,1,0:T(8,128)(2,1)}, bf16[4,2,96,512]{3,2,1,0:T(8,128)(2,1)S(1)}, u32[]{:S(2)}, u32[]{:S(2)}) collective-permute-start(bf16[4,2,96,512]{3,2,1,0:T(8,128)(2,1)} %tie.5.refs_2_.refs_3_), channel_id=1, source_target_pairs={{0,1},{1,0},{2,3},{3,2},{4,5},{5,4},{6,7},{7,6},{8,9},{9,8},{10,11... | collective-permute-start | bytes 2359304 | tf_op jit(solution)/shard_map/ppermute | solution.py:229
  43.3 25.7 %collective-permute-start.4 = (bf16[4,2,96,512]{3,2,1,0:T(8,128)(2,1)}, bf16[4,2,96,512]{3,2,1,0:T(8,128)(2,1)S(1)}, u32[]{:S(2)}, u32[]{:S(2)}) collective-permute-start(bf16[4,2,96,512]{3,2,1,0:T(8,128)(2,1)} %tie.5.refs_2_.refs_3_), channel_id=1, source_target_pairs={{0,4},{2,6},{4,0},{6,2},{8,12},{10,14},{12,8},{14,10},{16,20},{18,... | collective-permute-start | bytes 2359304 | tf_op jit(solution)/shard_map/ppermute | solution.py:229
  61.7 7.3 %copy-start.7 = (bf16[4,2,96,512]{3,2,1,0:T(8,128)(2,1)}, bf16[4,2,96,512]{3,2,1,0:T(8,128)(2,1)S(1)}, u32[]{:S(2)}) copy-start(bf16[4,2,96,512]{3,2,1,0:T(8,128)(2,1)S(1)} %collective-permute-done.5.refs_4_.refs_5_) | copy-start | bytes 2359300
  68.9 0.9 copy-start.9
  69.0 1.2 copy-start.6
  70.1 4.9 %copy-start.5 = (bf16[4,2,96,512]{3,2,1,0:T(8,128)(2,1)S(1)}, bf16[4,2,96,512]{3,2,1,0:T(8,128)(2,1)}, u32[]{:S(2)}) copy-start(bf16[4,2,96,512]{3,2,1,0:T(8,128)(2,1)} %tie.5.refs_2_.refs_3_) | copy-start | bytes 2359300
  70.1 5.4 %copy-start.8 = (bf16[4,2,96,512]{3,2,1,0:T(8,128)(2,1)S(1)}, bf16[4,2,96,512]{3,2,1,0:T(8,128)(2,1)}, u32[]{:S(2)}) copy-start(bf16[4,2,96,512]{3,2,1,0:T(8,128)(2,1)} %copy-done.7) | copy-start | bytes 2359300
  70.1 32.3 %all-to-all-start.2 = ((bf16[16,320,128]{2,1,0:T(8,128)(2,1)}), bf16[16,320,128]{2,1,0:T(8,128)(2,1)S(1)}, u32[]{:S(2)}, u32[]{:S(2)}) async-start(bf16[16,320,128]{2,1,0:T(8,128)(2,1)} %tie.6), calls=%async_computation.2 | async-start | bytes 2621440 | tf_op jit(solution)/shard_map/all_to_all | solution.py:351
  75.0 6.0 %copy-start.10 = (bf16[4,2,96,512]{3,2,1,0:T(8,128)(2,1)S(1)}, bf16[4,2,96,512]{3,2,1,0:T(8,128)(2,1)}, u32[]{:S(2)}) copy-start(bf16[4,2,96,512]{3,2,1,0:T(8,128)(2,1)} %copy-done.9) | copy-start | bytes 2359300
  75.0 15.9 %collective-permute-start.8 = (bf16[4,2,96,512]{3,2,1,0:T(8,128)(2,1)S(1)}, bf16[4,2,96,512]{3,2,1,0:T(8,128)(2,1)}, u32[]{:S(2)}, u32[]{:S(2)}) collective-permute-start(bf16[4,2,96,512]{3,2,1,0:T(8,128)(2,1)S(1)} %copy-done.5), channel_id=1, source_target_pairs={{0,2},{2,0},{4,6},{6,4},{8,10},{10,8},{12,14},{14,12},{16,18},{18,... | collective-permute-start | bytes 2359304 | tf_op jit(solution)/shard_map/ppermute | solution.py:229
  75.5 22.7 %collective-permute-start.10 = (bf16[4,2,96,512]{3,2,1,0:T(8,128)(2,1)S(1)}, bf16[4,2,96,512]{3,2,1,0:T(8,128)(2,1)}, u32[]{:S(2)}, u32[]{:S(2)}) collective-permute-start(bf16[4,2,96,512]{3,2,1,0:T(8,128)(2,1)S(1)} %copy-done.8), channel_id=1, source_target_pairs={{0,2},{2,0},{4,6},{6,4},{8,10},{10,8},{12,14},{14,12},{16,18},{18,... | collective-permute-start | bytes 2359304 | tf_op jit(solution)/shard_map/ppermute | solution.py:229
  75.6 22.6 %collective-permute-start.9 = (bf16[4,2,96,512]{3,2,1,0:T(8,128)(2,1)}, bf16[4,2,96,512]{3,2,1,0:T(8,128)(2,1)}, u32[]{:S(2)}, u32[]{:S(2)}) collective-permute-start(bf16[4,2,96,512]{3,2,1,0:T(8,128)(2,1)} %copy-done.9), channel_id=1, source_target_pairs={{0,2},{2,0},{4,6},{6,4},{8,10},{10,8},{12,14},{14,12},{16,18},{18,... | collective-permute-start | bytes 2359304 | tf_op jit(solution)/shard_map/ppermute | solution.py:229
  77.0 8.4 %collective-permute-start = (bf16[30,8,512]{2,0,1:T(8,128)(2,1)S(1)}, bf16[30,8,512]{2,0,1:T(8,128)(2,1)S(1)}, u32[]{:S(2)}, u32[]{:S(2)}) collective-permute-start(bf16[30,8,512]{2,0,1:T(8,128)(2,1)S(1)} %bitcast.57), channel_id=1, source_target_pairs={{0,1},{1,0},{2,3},{3,2},{4,5},{5,4},{6,7},{7,6},{8,9},{9,8},{10,11... | collective-permute-start | bytes 737288 | tf_op jit(solution)/shard_map/ppermute | solution.py:265
  79.3 18.8 %collective-permute-start.6 = (bf16[4,1,96,512]{3,2,1,0:T(8,128)(2,1)}, bf16[4,1,96,512]{3,2,1,0:T(8,128)(2,1)}, u32[]{:S(2)}, u32[]{:S(2)}) collective-permute-start(bf16[4,1,96,512]{3,2,1,0:T(8,128)(2,1)} %slice.8), channel_id=1, source_target_pairs={{0,4},{2,6},{4,0},{6,2},{8,12},{10,14},{12,8},{14,10},{16,20},{18,... | collective-permute-start | bytes 1179656 | tf_op jit(solution)/shard_map/ppermute | solution.py:229
  85.4 0.7 copy-start.18
  86.1 12.1 %collective-permute-start.7 = (bf16[4,1,96,512]{3,2,1,0:T(8,128)(2,1)}, bf16[4,1,96,512]{3,2,1,0:T(8,128)(2,1)}, u32[]{:S(2)}, u32[]{:S(2)}) collective-permute-start(bf16[4,1,96,512]{3,2,1,0:T(8,128)(2,1)} %slice.9), channel_id=1, source_target_pairs={{0,1},{1,0},{2,3},{3,2},{4,5},{5,4},{6,7},{7,6},{8,9},{9,8},{10,11... | collective-permute-start | bytes 1179656 | tf_op jit(solution)/shard_map/ppermute | solution.py:229
  102.4 1.1 copy-start.4
  103.5 31.0 %all-to-all-start.3 = ((bf16[16,256,128]{2,1,0:T(8,128)(2,1)}), bf16[16,256,128]{2,1,0:T(8,128)(2,1)S(1)}, u32[]{:S(2)}, u32[]{:S(2)}) async-start(bf16[16,256,128]{2,1,0:T(8,128)(2,1)} %tie.7), calls=%async_computation.3 | async-start | bytes 2097152 | tf_op jit(solution)/shard_map/all_to_all | solution.py:351
  111.6 2.0 %collective-permute-start.11 = (bf16[4,1,96,512]{3,2,1,0:T(8,128)(2,1)}, bf16[4,1,96,512]{3,2,1,0:T(8,128)(2,1)S(1)}, u32[]{:S(2)}, u32[]{:S(2)}) collective-permute-start(bf16[4,1,96,512]{3,2,1,0:T(8,128)(2,1)} %collective-permute-done.6.refs_5_.refs_3_.refs_6_), channel_id=1, source_target_pairs={{0,2},{2,0},{4,6},{6,4},{8,10},{10,8},{12,14},{14,12},{16,18},{18,... | collective-permute-start | bytes 1179656 | tf_op jit(solution)/shard_map/ppermute | solution.py:229
  112.0 2.1 %collective-permute-start.12 = (bf16[4,1,96,512]{3,2,1,0:T(8,128)(2,1)}, bf16[4,1,96,512]{3,2,1,0:T(8,128)(2,1)S(1)}, u32[]{:S(2)}, u32[]{:S(2)}) collective-permute-start(bf16[4,1,96,512]{3,2,1,0:T(8,128)(2,1)} %collective-permute-done.7.refs_6_.refs_4_.refs_7_), channel_id=1, source_target_pairs={{0,2},{2,0},{4,6},{6,4},{8,10},{10,8},{12,14},{14,12},{16,18},{18,... | collective-permute-start | bytes 1179656 | tf_op jit(solution)/shard_map/ppermute | solution.py:229
  113.6 0.8 copy-start.19
  114.2 0.8 copy-start.20
  134.5 1.0 copy-start.11
where the time goes:
time: 152 us; the launch traced here: 150 us
  Pallas kernels  48 us (32%)
  waiting for transfers between devices  40.3 us (27%)
  starting transfers between devices  32.5 us (21%)
  blocking collectives  12.4 us (8%)
  local copies, waits for them, and re-layouts  11.2 us (7%)
  other arithmetic  3.04 us (2%)
  between operations  2.32 us (2%)
    pallas_call x2, Pallas kernels, local(): pl.pallas_call(functools.partial(stage_kernel, part, len(filters), first,...  27.6 us
    ppermute x12, waiting for transfers between devices, swapped(): return lax.ppermute(array, axis, pairs)  26.5 us
    pallas_call x3, Pallas kernels, local(): pl.pallas_call(functools.partial(gather_kernel, capacity, cuts[number]),...  19.1 us
    all_to_all x3, starting transfers between devices, local(): lax.all_to_all(rows, 'table', split_axis=0, concat_axis=0, tiled=True)  16.7 us
    ppermute x12, starting transfers between devices, swapped(): return lax.ppermute(array, axis, pairs)  14.3 us
    all_to_all x1, blocking collectives, local(): lax.all_to_all(requests, 'table', split_axis=0, concat_axis=0, tiled=True)  12.4 us
    all_to_all x3, waiting for transfers between devices, local(): lax.all_to_all(rows, 'table', split_axis=0, concat_axis=0, tiled=True)  10.3 us
    unnamed x43, local copies, waits for them, and re-layouts  9.6 us
  transfers between devices with their start and end apart: 16, of which 9 were waited for; matrix products, arithmetic and copies ran while one was open for 4% of the time, Pallas kernels for 23%

commit v1 on v0

--- a/solution.py
+++ b/solution.py
@@ -9,7 +9,7 @@
 table_of_id = (0, 1, 2, 2, 3, 3, 3, 3)
 bag_bounds = ((0, 1), (1, 2), (2, 4), (4, 8))
 epsilon = 1e-05
-part_ends = (0.25, 2 / 3, 1.0)
+part_ends = (0.25, 0.75, 1.0)
 stage_parts = (2, 3)
 megabyte = 1024 * 1024
 
@@ -230,9 +230,9 @@
 
 
 def block_place(number, side):
-    kind = number % 5
-    bits = (2 if kind in (1, 3, 4) else 0) + number // 5
-    base = 2 * (side if kind < 2 else 1 - side) + (1 if kind == 4 else 0)
+    kind = number % 6
+    bits = (2 if kind > 1 else 0) + number // 6
+    base = 2 * (side if kind in (0, 2, 3) else 1 - side) + (1 if kind in (3, 5) else 0)
     return bits, base
 
 
@@ -312,7 +312,9 @@
     for number in range(len(part_ends)):
         piece = cuts[number + 1] - cuts[number]
         if number == 1:
-            line = line + [swapped(line[middle], "table", 4 * step) for step in range(1, middle)]
+            middle_shard = tie(line[middle], received)
+            line = line + [swapped(middle_shard, "table", 4 * step) for step in range(1, middle)]
+            line[middle] = middle_shard
             sent[0] = tie(sent[0], *line[middle + 1 :])
         earlier = sent[-1:] if sent else line[1:]
         sent.append(
@@ -339,19 +341,21 @@
             )(received, flat_table, *earlier)
         )
     line = tie(jnp.stack(line), sent[0])
-    by_table = swapped(line, "table", 2)
     by_rep = swapped(line, "rep", 1)
-    corner_low = swapped(by_rep[:, : half // 2], "table", 2)
-    corner_high = swapped(by_table[:, half // 2 :], "rep", 1)
-    near = [swapped(block, "table", 1) for block in (line, by_table, by_rep)]
-    gates = [[], [sent[2], by_table, by_rep], [state, corner_low, corner_high] + near]
+    table_low = swapped(line[:, : half // 2], "table", 2)
+    table_high = swapped(line[:, half // 2 :], "table", 2)
+    corner_low = swapped(table_low, "rep", 1)
+    corner_high = swapped(table_high, "rep", 1)
+    near = [swapped(block, "table", 1) for block in (line, by_rep, table_low)]
+    gates = [[], [sent[2], by_rep, table_low], [state, corner_low, corner_high] + near]
     for rows, gate in zip(sent, gates):
         if returned:
             rows = tie(rows, returned[-1], *gate)
         arrived = lax.all_to_all(rows, "table", split_axis=0, concat_axis=0, tiled=True)
         returned.append(arrived.reshape(-1, row_width))
-    near = near + [swapped(block, "table", 1) for block in (corner_low, corner_high)]
-    filters = [line, by_table, by_rep, corner_low, corner_high] + near
+    late = [table_high, corner_low, corner_high]
+    filters = [line, by_rep, table_low] + late + near
+    filters = filters + [swapped(block, "table", 1) for block in late]
     if conv_weight.shape[1] % 16:
         filters = [ordered_filters(filters, me)]
     weight_by_slot = bag_weight.reshape(token_count, bag_width).T
@@ -378,7 +382,7 @@
                 pltpu.VMEM((slots + 16, channels), jnp.float32),
                 pltpu.VMEM((slots + 16, channels), jnp.float32),
                 pltpu.VMEM((slots, channels), jnp.bfloat16),
-                pltpu.SemaphoreType.DMA((10 * (owners // 4),)),
+                pltpu.SemaphoreType.DMA((12 * (owners // 4),)),
                 pltpu.SemaphoreType.DMA(((slots + 255) // 256,)),
             ],
             input_output_aliases={5 + part + len(filters): 0} if known else {},

time: 152 us -> 151 us (level); the launches traced: 150 us -> 150 us
  blocking collectives: 12.4 us -> 10 us
    ppermute x12 -> x14, waiting for transfers between devices: 26.5 us -> 40.9 us  [swapped(): return lax.ppermute(array, axis, pairs)]
    all_to_all x3, waiting for transfers between devices: 10.3 us -> 0.01 us  [local(): lax.all_to_all(rows, 'table', split_axis=0, concat_axis=0, tiled=True)]
    ppermute x1, waiting for transfers between devices: 3.57 us -> 0.01 us  [carried_rows(): arrived = lax.ppermute(by_position, 'rep', pairs)]
    all_to_all x1, blocking collectives: 12.4 us -> 10 us  [local(): lax.all_to_all(requests, 'table', split_axis=0, concat_axis=0, tiled=True)]
    unnamed x43 -> x45, local copies, waits for them, and re-layouts: 9.6 us -> 10.4 us
    ppermute x12 -> x14, starting transfers between devices: 14.3 us -> 14.7 us  [swapped(): return lax.ppermute(array, axis, pairs)]
  transfers between devices with their start and end apart: 16 -> 18, of which waited for: 9 -> 9; matrix products, arithmetic and copies ran while one was open for 4% -> 4% of each run, Pallas kernels for 23% -> 20%
where the time goes in v1:
time: 151 us; the launch traced here: 150 us
  Pallas kernels  49.2 us (33%)
  waiting for transfers between devices  41 us (27%)
  starting transfers between devices  32.6 us (22%)
  local copies, waits for them, and re-layouts  12.4 us (8%)
  blocking collectives  10 us (7%)
  other arithmetic  2.97 us (2%)
  between operations  2.36 us (2%)
    ppermute x14, waiting for transfers between devices, swapped(): return lax.ppermute(array, axis, pairs)  40.9 us
    pallas_call x2, Pallas kernels, local(): pl.pallas_call(functools.partial(stage_kernel, part, len(filters), first,...  28.9 us
    pallas_call x3, Pallas kernels, local(): pl.pallas_call(functools.partial(gather_kernel, capacity, cuts[number]),...  19.1 us
    all_to_all x3, starting transfers between devices, local(): lax.all_to_all(rows, 'table', split_axis=0, concat_axis=0, tiled=True)  16.4 us
    ppermute x14, starting transfers between devices, swapped(): return lax.ppermute(array, axis, pairs)  14.7 us
    unnamed x45, local copies, waits for them, and re-layouts  10.4 us
    all_to_all x1, blocking collectives, local(): lax.all_to_all(requests, 'table', split_axis=0, concat_axis=0, tiled=True)  10 us
  transfers between devices with their start and end apart: 18, of which 9 were waited for; matrix products, arithmetic and copies ran while one was open for 4% of the time, Pallas kernels for 20%

profile of v1, /device:TPU:0, one launch (start us, length us, event | category | flops | bytes accessed | tf_op | source)
XLA Modules:
  0.0 150.5 jit_solution(4957587426715776681)
XLA Ops:
  0.0 1.0 copy-done
  1.0 4.1 %collective-permute-start.2 = (bf16[2,96,512]{2,1,0:T(8,128)(2,1)S(1)}, bf16[2,96,512]{2,1,0:T(8,128)(2,1)S(1)}, u32[]{:S(2)}, u32[]{:S(2)}) collective-permute-start(bf16[2,96,512]{2,1,0:T(8,128)(2,1)S(1)} %constant_dynamic-slice_fusion), channel_id=1, source_target_pairs={{0,16},{2,18},{4,20},{6,22},{8,24},{10,26},{12,28},{14,30},{16,0},... | collective-permute-start | bytes 589832 | tf_op jit(solution)/shard_map/ppermute | solution.py:229
  5.1 1.6 %collective-permute-start.1 = (bf16[2,96,512]{2,1,0:T(8,128)(2,1)S(1)}, bf16[2,96,512]{2,1,0:T(8,128)(2,1)S(1)}, u32[]{:S(2)}, u32[]{:S(2)}) collective-permute-start(bf16[2,96,512]{2,1,0:T(8,128)(2,1)S(1)} %constant_dynamic-slice_fusion), channel_id=1, source_target_pairs={{0,8},{2,10},{4,12},{6,14},{8,0},{10,2},{12,4},{14,6},{16,24},{18,... | collective-permute-start | bytes 589832 | tf_op jit(solution)/shard_map/ppermute | solution.py:229
  6.7 0.8 copy-done.2
  7.5 0.8 copy-done.3
  8.2 1.2 prep.1
  9.5 10.0 %all_to_all.20 = s32[16,1,768]{2,1,0:T(1,128)} all-to-all(s32[16,1,768]{2,1,0:T(1,128)S(1)} %get-tuple-element.11), channel_id=1, replica_groups=mesh['table'=16,'rep'=2] {'table'}, dimensions={0} | all-to-all | bytes 98304 | tf_op jit(solution)/shard_map/all_to_all | solution.py:307
  19.5 0.7 copy-done.10
  20.3 5.4 %owner_gather.3.refs_0_ = bf16[16,192,128]{2,1,0:T(8,128)(2,1)} custom-call(s32[12288]{0:T(1024)} %bitcast.52, bf16[8192,128]{1,0:T(8,128)(2,1)} %bitcast.41, bf16[2,96,512]{2,1,0:T(8,128)(2,1)} %copy-done.13, bf16[2,96,512]{2,1,0:T(8,128)(2,1)} %copy-done.10), custom_call_target="tpu_custom_call" | custom-call | bytes 20971520 | tf_op jit(solution)/shard_map/owner_gather/pallas_call | solution.py:321
  25.7 0.3 collective-permute-start.3
  26.0 6.4 %collective-permute-done.3.refs_1_ = bf16[2,96,512]{2,1,0:T(8,128)(2,1)S(1)} collective-permute-done((bf16[2,96,512]{2,1,0:T(8,128)(2,1)}, bf16[2,96,512]{2,1,0:T(8,128)(2,1)S(1)}, u32[]{:S(2)}, u32[]{:S(2)}) %collective-permute-start.3) | collective-permute-done | bytes 196640 | tf_op jit(solution)/shard_map/ppermute | solution.py:229
  32.4 0.7 copy-done.15
  33.1 3.7 %all-to-all-start.1 = ((bf16[16,192,128]{2,1,0:T(8,128)(2,1)}), bf16[16,192,128]{2,1,0:T(8,128)(2,1)S(1)}, u32[]{:S(2)}, u32[]{:S(2)}) async-start(bf16[16,192,128]{2,1,0:T(8,128)(2,1)} %tie.6.refs_0_.refs_1_), calls=%async_computation.1 | async-start | bytes 1572864 | tf_op jit(solution)/shard_map/all_to_all | solution.py:354
  36.9 1.0 pad_maximum_fusion.refs_0_
  37.9 1.5 collective-permute-start.4
  39.4 2.0 %fusion.1 = (bf16[4,1,96,512]{3,2,1,0:T(8,128)(2,1)}, bf16[4,1,96,512]{3,2,1,0:T(8,128)(2,1)S(1)}) fusion(bf16[4,2,96,512]{3,2,1,0:T(8,128)(2,1)} %tie.7.refs_2_.refs_3_), kind=kLoop, calls=%fused_computation.6 | loop fusion | bytes 1572864 | tf_op jit(solution)/shard_map/slice | solution.py:346
  41.3 1.8 %collective-permute-start.5 = (bf16[4,1,96,512]{3,2,1,0:T(8,128)(2,1)S(1)}, bf16[4,1,96,512]{3,2,1,0:T(8,128)(2,1)S(1)}, u32[]{:S(2)}, u32[]{:S(2)}) collective-permute-start(bf16[4,1,96,512]{3,2,1,0:T(8,128)(2,1)S(1)} %get-tuple-element.16), channel_id=1, source_target_pairs={{0,4},{2,6},{4,0},{6,2},{8,12},{10,14},{12,8},{14,10},{16,20},{18,... | collective-permute-start | bytes 1179656 | tf_op jit(solution)/shard_map/ppermute | solution.py:229
  43.1 8.3 %owner_gather.4.refs_0_ = bf16[16,384,128]{2,1,0:T(8,128)(2,1)} custom-call(s32[12288]{0:T(1024)} %bitcast.54, bf16[8192,128]{1,0:T(8,128)(2,1)} %bitcast.42, bf16[16,192,128]{2,1,0:T(8,128)(2,1)} %tie.6.refs_0_.refs_1_), custom_call_target="tpu_custom_call" | custom-call | bytes 20971520 | tf_op jit(solution)/shard_map/owner_gather/pallas_call | solution.py:321
  51.4 5.4 %owner_gather.5.refs_2_.refs_0_ = bf16[16,192,128]{2,1,0:T(8,128)(2,1)} custom-call(s32[12288]{0:T(1024)} %bitcast.55, bf16[8192,128]{1,0:T(8,128)(2,1)} %bitcast.43, bf16[16,384,128]{2,1,0:T(8,128)(2,1)} %owner_gather.4.refs_0_), custom_call_target="tpu_custom_call" | custom-call | bytes 20971520 | tf_op jit(solution)/shard_map/owner_gather/pallas_call | solution.py:321
  56.9 0.9 collective-permute-done.4.refs_3_.refs_4_
  57.8 0.9 copy-done.8
  58.7 0.3 copy-done.6
  58.9 6.0 %all-to-all-start.2 = ((bf16[16,384,128]{2,1,0:T(8,128)(2,1)}), bf16[16,384,128]{2,1,0:T(8,128)(2,1)S(1)}, u32[]{:S(2)}, u32[]{:S(2)}) async-start(bf16[16,384,128]{2,1,0:T(8,128)(2,1)} %tie.8), calls=%async_computation.2 | async-start | bytes 3145728 | tf_op jit(solution)/shard_map/all_to_all | solution.py:354
  64.9 1.9 %collective-permute-start.6 = (bf16[4,1,96,512]{3,2,1,0:T(8,128)(2,1)}, bf16[4,1,96,512]{3,2,1,0:T(8,128)(2,1)}, u32[]{:S(2)}, u32[]{:S(2)}) collective-permute-start(bf16[4,1,96,512]{3,2,1,0:T(8,128)(2,1)} %get-tuple-element.15), channel_id=1, source_target_pairs={{0,4},{2,6},{4,0},{6,2},{8,12},{10,14},{12,8},{14,10},{16,20},{18,... | collective-permute-start | bytes 1179656 | tf_op jit(solution)/shard_map/ppermute | solution.py:229
  66.8 0.5 collective-permute-start.10
  67.4 1.0 copy.22
  68.4 0.7 copy-done.20
  69.1 1.5 collective-permute-start
  70.6 18.6 %collective-permute-done.6.refs_5_.refs_6_ = bf16[4,1,96,512]{3,2,1,0:T(8,128)(2,1)} collective-permute-done((bf16[4,1,96,512]{3,2,1,0:T(8,128)(2,1)}, bf16[4,1,96,512]{3,2,1,0:T(8,128)(2,1)}, u32[]{:S(2)}, u32[]{:S(2)}) %collective-permute-start.6) | collective-permute-done | bytes 393248 | tf_op jit(solution)/shard_map/ppermute | solution.py:229
  89.2 1.5 collective-permute-start.8
  90.7 0.7 copy-done.21
  91.4 0.5 collective-permute-start.7
  93.9 1.4 fusion.carried_ref.refs_2_
  95.3 6.2 %collective-permute-done.8.refs_7_.refs_4_.refs_8_ = bf16[4,1,96,512]{3,2,1,0:T(8,128)(2,1)} collective-permute-done((bf16[4,1,96,512]{3,2,1,0:T(8,128)(2,1)}, bf16[4,1,96,512]{3,2,1,0:T(8,128)(2,1)}, u32[]{:S(2)}, u32[]{:S(2)}) %collective-permute-start.8) | collective-permute-done | bytes 393248 | tf_op jit(solution)/shard_map/ppermute | solution.py:229
  101.6 7.2 %collective-permute-done.7.refs_6_.refs_3_.refs_7_ = bf16[4,1,96,512]{3,2,1,0:T(8,128)(2,1)} collective-permute-done((bf16[4,1,96,512]{3,2,1,0:T(8,128)(2,1)}, bf16[4,1,96,512]{3,2,1,0:T(8,128)(2,1)}, u32[]{:S(2)}, u32[]{:S(2)}) %collective-permute-start.7) | collective-permute-done | bytes 393248 | tf_op jit(solution)/shard_map/ppermute | solution.py:229
  108.7 1.2 copy-done.4
  109.9 6.7 %all-to-all-start.3 = ((bf16[16,192,128]{2,1,0:T(8,128)(2,1)}), bf16[16,192,128]{2,1,0:T(8,128)(2,1)S(1)}, u32[]{:S(2)}, u32[]{:S(2)}) async-start(bf16[16,192,128]{2,1,0:T(8,128)(2,1)} %tie.9), calls=%async_computation.3 | async-start | bytes 1572864 | tf_op jit(solution)/shard_map/all_to_all | solution.py:354
  116.6 0.5 collective-permute-start.12
  117.2 0.4 collective-permute-start.13
  117.6 0.6 pad_add_fusion.me_ref
  118.1 0.5 collective-permute-done.12.refs_11_.refs_12_
  118.6 0.6 collective-permute-done.14.refs_13_.refs_14_
  119.2 0.6 collective-permute-done.13.refs_12_.refs_13_
  119.7 0.2 copy-done.18
  119.9 0.6 copy-done.19
  120.5 15.6 %stage.2 = (bf16[1024,512]{1,0:T(8,128)(2,1)}, f32[30,512]{1,0:T(8,128)}) custom-call(s32[8,1024]{1,0:T(8,128)} %copy-done.1, s32[2]{0:T(128)} %pad_add_fusion.me_ref, f32[8,1024]{1,0:T(8,128)} %bitcast.59, f32[30,512]{1,0:T(8,128)} %fusion.carried_ref.refs_2_, f32[4,512]{1,0:T(4,128)} %gain_ref.3, bf16[3072,128]{1,0:T(8,128)(2,1)} %bitcast.48, ...), custom_call_target="tpu_custom_call" | custom-call | flops 3623878656 | bytes 25165824 | tf_op jit(solution)/shard_map/stage/pallas_call | solution.py:368
  136.2 0.9 copy-done.7
  137.1 13.2 %stage.3 = (bf16[1024,512]{1,0:T(8,128)(2,1)}, f32[30,512]{1,0:T(8,128)}) custom-call(s32[8,1024]{1,0:T(8,128)} %copy-done.1, s32[2]{0:T(128)} %pad_add_fusion.me_ref, f32[8,1024]{1,0:T(8,128)} %bitcast.60, f32[30,512]{1,0:T(8,128)} %get-tuple-element.12.carried_ref, f32[4,512]{1,0:T(4,128)} %gain_ref.3, ...), custom_call_target="tpu_custom_call", output_to_operand_aliasing={{0}: (20, {})} | custom-call | flops 2818572288 | bytes 25165824 | tf_op jit(solution)/shard_map/stage/pallas_call | solution.py:368
  (51 shorter events, 0.4 us)
Async XLA Ops:
  0.0 1.0 copy-start
  1.0 18.5 %collective-permute-start.2 = (bf16[2,96,512]{2,1,0:T(8,128)(2,1)S(1)}, bf16[2,96,512]{2,1,0:T(8,128)(2,1)S(1)}, u32[]{:S(2)}, u32[]{:S(2)}) collective-permute-start(bf16[2,96,512]{2,1,0:T(8,128)(2,1)S(1)} %constant_dynamic-slice_fusion), channel_id=1, source_target_pairs={{0,16},{2,18},{4,20},{6,22},{8,24},{10,26},{12,28},{14,30},{16,0},... | collective-permute-start | bytes 589832 | tf_op jit(solution)/shard_map/ppermute | solution.py:229
  5.1 14.4 %collective-permute-start.1 = (bf16[2,96,512]{2,1,0:T(8,128)(2,1)S(1)}, bf16[2,96,512]{2,1,0:T(8,128)(2,1)S(1)}, u32[]{:S(2)}, u32[]{:S(2)}) collective-permute-start(bf16[2,96,512]{2,1,0:T(8,128)(2,1)S(1)} %constant_dynamic-slice_fusion), channel_id=1, source_target_pairs={{0,8},{2,10},{4,12},{6,14},{8,0},{10,2},{12,4},{14,6},{16,24},{18,... | collective-permute-start | bytes 589832 | tf_op jit(solution)/shard_map/ppermute | solution.py:229
  6.7 0.8 copy-start.2
  7.5 0.8 copy-start.3
  9.5 10.0 %copy-start.1 = (s32[8,1024]{1,0:T(8,128)}, s32[8,1024]{1,0:T(8,128)S(1)}, u32[]{:S(2)}) copy-start(s32[8,1024]{1,0:T(8,128)S(1)} %get-tuple-element.10.place_ref) | copy-start | bytes 98308
  19.5 0.7 copy-start.10
  19.5 0.7 copy-start.13
  25.7 11.2 %copy-start.11 = (bf16[2,96,512]{2,1,0:T(8,128)(2,1)S(1)}, bf16[2,96,512]{2,1,0:T(8,128)(2,1)}, u32[]{:S(2)}) copy-start(bf16[2,96,512]{2,1,0:T(8,128)(2,1)} %tie.5) | copy-start | bytes 589828
  25.7 11.2 %copy-start.14 = (bf16[2,96,512]{2,1,0:T(8,128)(2,1)S(1)}, bf16[2,96,512]{2,1,0:T(8,128)(2,1)}, u32[]{:S(2)}) copy-start(bf16[2,96,512]{2,1,0:T(8,128)(2,1)} %copy-done.13) | copy-start | bytes 589828
  25.7 6.7 %collective-permute-start.3 = (bf16[2,96,512]{2,1,0:T(8,128)(2,1)}, bf16[2,96,512]{2,1,0:T(8,128)(2,1)S(1)}, u32[]{:S(2)}, u32[]{:S(2)}) collective-permute-start(bf16[2,96,512]{2,1,0:T(8,128)(2,1)} %tie.5), channel_id=1, source_target_pairs={{0,8},{2,10},{4,12},{6,14},{8,0},{10,2},{12,4},{14,6},{16,24},{18,... | collective-permute-start | bytes 589832 | tf_op jit(solution)/shard_map/ppermute | solution.py:229
  32.4 0.7 copy-start.15
  33.1 3.8 %copy-start.16 = (bf16[2,96,512]{2,1,0:T(8,128)(2,1)S(1)}, bf16[2,96,512]{2,1,0:T(8,128)(2,1)}, u32[]{:S(2)}) copy-start(bf16[2,96,512]{2,1,0:T(8,128)(2,1)} %copy-done.15) | copy-start | bytes 589828
  33.1 24.7 %all-to-all-start.1 = ((bf16[16,192,128]{2,1,0:T(8,128)(2,1)}), bf16[16,192,128]{2,1,0:T(8,128)(2,1)S(1)}, u32[]{:S(2)}, u32[]{:S(2)}) async-start(bf16[16,192,128]{2,1,0:T(8,128)(2,1)} %tie.6.refs_0_.refs_1_), calls=%async_computation.1 | async-start | bytes 1572864 | tf_op jit(solution)/shard_map/all_to_all | solution.py:354
  37.9 19.9 %collective-permute-start.4 = (bf16[4,2,96,512]{3,2,1,0:T(8,128)(2,1)}, bf16[4,2,96,512]{3,2,1,0:T(8,128)(2,1)S(1)}, u32[]{:S(2)}, u32[]{:S(2)}) collective-permute-start(bf16[4,2,96,512]{3,2,1,0:T(8,128)(2,1)} %tie.7.refs_2_.refs_3_), channel_id=1, source_target_pairs={{0,1},{1,0},{2,3},{3,2},{4,5},{5,4},{6,7},{7,6},{8,9},{9,8},{10,11... | collective-permute-start | bytes 2359304 | tf_op jit(solution)/shard_map/ppermute | solution.py:229
  41.3 15.6 %collective-permute-start.5 = (bf16[4,1,96,512]{3,2,1,0:T(8,128)(2,1)S(1)}, bf16[4,1,96,512]{3,2,1,0:T(8,128)(2,1)S(1)}, u32[]{:S(2)}, u32[]{:S(2)}) collective-permute-start(bf16[4,1,96,512]{3,2,1,0:T(8,128)(2,1)S(1)} %get-tuple-element.16), channel_id=1, source_target_pairs={{0,4},{2,6},{4,0},{6,2},{8,12},{10,14},{12,8},{14,10},{16,20},{18,... | collective-permute-start | bytes 1179656 | tf_op jit(solution)/shard_map/ppermute | solution.py:229
  56.9 0.9 copy-start.12
  57.8 0.9 copy-start.8
  57.8 1.1 copy-start.6
  58.9 7.9 %copy-start.5 = (bf16[4,2,96,512]{3,2,1,0:T(8,128)(2,1)S(1)}, bf16[4,2,96,512]{3,2,1,0:T(8,128)(2,1)}, u32[]{:S(2)}) copy-start(bf16[4,2,96,512]{3,2,1,0:T(8,128)(2,1)} %tie.7.refs_2_.refs_3_) | copy-start | bytes 2359300
  58.9 7.9 %copy-start.9 = (bf16[4,2,96,512]{3,2,1,0:T(8,128)(2,1)S(1)}, bf16[4,2,96,512]{3,2,1,0:T(8,128)(2,1)}, u32[]{:S(2)}) copy-start(bf16[4,2,96,512]{3,2,1,0:T(8,128)(2,1)} %copy-done.8) | copy-start | bytes 2359300
  58.9 49.8 %all-to-all-start.2 = ((bf16[16,384,128]{2,1,0:T(8,128)(2,1)}), bf16[16,384,128]{2,1,0:T(8,128)(2,1)S(1)}, u32[]{:S(2)}, u32[]{:S(2)}) async-start(bf16[16,384,128]{2,1,0:T(8,128)(2,1)} %tie.8), calls=%async_computation.2 | async-start | bytes 3145728 | tf_op jit(solution)/shard_map/all_to_all | solution.py:354
  64.9 24.3 %collective-permute-start.6 = (bf16[4,1,96,512]{3,2,1,0:T(8,128)(2,1)}, bf16[4,1,96,512]{3,2,1,0:T(8,128)(2,1)}, u32[]{:S(2)}, u32[]{:S(2)}) collective-permute-start(bf16[4,1,96,512]{3,2,1,0:T(8,128)(2,1)} %get-tuple-element.15), channel_id=1, source_target_pairs={{0,4},{2,6},{4,0},{6,2},{8,12},{10,14},{12,8},{14,10},{16,20},{18,... | collective-permute-start | bytes 1179656 | tf_op jit(solution)/shard_map/ppermute | solution.py:229
  66.8 41.9 %collective-permute-start.9 = (bf16[4,2,96,512]{3,2,1,0:T(8,128)(2,1)S(1)}, bf16[4,2,96,512]{3,2,1,0:T(8,128)(2,1)}, u32[]{:S(2)}, u32[]{:S(2)}) collective-permute-start(bf16[4,2,96,512]{3,2,1,0:T(8,128)(2,1)S(1)} %copy-done.5), channel_id=1, source_target_pairs={{0,2},{2,0},{4,6},{6,4},{8,10},{10,8},{12,14},{14,12},{16,18},{18,... | collective-permute-start | bytes 2359304 | tf_op jit(solution)/shard_map/ppermute | solution.py:229
  66.8 41.9 %collective-permute-start.10 = (bf16[4,2,96,512]{3,2,1,0:T(8,128)(2,1)S(1)}, bf16[4,2,96,512]{3,2,1,0:T(8,128)(2,1)}, u32[]{:S(2)}, u32[]{:S(2)}) collective-permute-start(bf16[4,2,96,512]{3,2,1,0:T(8,128)(2,1)S(1)} %copy-done.9), channel_id=1, source_target_pairs={{0,2},{2,0},{4,6},{6,4},{8,10},{10,8},{12,14},{14,12},{16,18},{18,... | collective-permute-start | bytes 2359304 | tf_op jit(solution)/shard_map/ppermute | solution.py:229
  68.4 0.7 copy-start.20
  69.1 21.6 %collective-permute-start = (bf16[30,8,512]{2,0,1:T(8,128)(2,1)S(1)}, bf16[30,8,512]{2,0,1:T(8,128)(2,1)S(1)}, u32[]{:S(2)}, u32[]{:S(2)}) collective-permute-start(bf16[30,8,512]{2,0,1:T(8,128)(2,1)S(1)} %bitcast.58), channel_id=1, source_target_pairs={{0,1},{1,0},{2,3},{3,2},{4,5},{5,4},{6,7},{7,6},{8,9},{9,8},{10,11... | collective-permute-start | bytes 737288 | tf_op jit(solution)/shard_map/ppermute | solution.py:265
  70.6 31.0 %collective-permute-start.11 = (bf16[4,1,96,512]{3,2,1,0:T(8,128)(2,1)}, bf16[4,1,96,512]{3,2,1,0:T(8,128)(2,1)}, u32[]{:S(2)}, u32[]{:S(2)}) collective-permute-start(bf16[4,1,96,512]{3,2,1,0:T(8,128)(2,1)} %copy-done.12), channel_id=1, source_target_pairs={{0,2},{2,0},{4,6},{6,4},{8,10},{10,8},{12,14},{14,12},{16,18},{18,... | collective-permute-start | bytes 1179656 | tf_op jit(solution)/shard_map/ppermute | solution.py:229
  89.2 12.3 %collective-permute-start.8 = (bf16[4,1,96,512]{3,2,1,0:T(8,128)(2,1)}, bf16[4,1,96,512]{3,2,1,0:T(8,128)(2,1)}, u32[]{:S(2)}, u32[]{:S(2)}) collective-permute-start(bf16[4,1,96,512]{3,2,1,0:T(8,128)(2,1)} %collective-permute-done.6.refs_5_.refs_6_), channel_id=1, source_target_pairs={{0,1},{1,0},{2,3},{3,2},{4,5},{5,4},{6,7},{7,6},{8,9},{9,8},{10,11... | collective-permute-start | bytes 1179656 | tf_op jit(solution)/shard_map/ppermute | solution.py:229
  90.7 0.7 copy-start.21
  91.4 17.3 %collective-permute-start.7 = (bf16[4,1,96,512]{3,2,1,0:T(8,128)(2,1)}, bf16[4,1,96,512]{3,2,1,0:T(8,128)(2,1)}, u32[]{:S(2)}, u32[]{:S(2)}) collective-permute-start(bf16[4,1,96,512]{3,2,1,0:T(8,128)(2,1)} %copy-done.12), channel_id=1, source_target_pairs={{0,1},{1,0},{2,3},{3,2},{4,5},{5,4},{6,7},{7,6},{8,9},{9,8},{10,11... | collective-permute-start | bytes 1179656 | tf_op jit(solution)/shard_map/ppermute | solution.py:229
  108.7 1.2 copy-start.4
  109.9 26.2 %all-to-all-start.3 = ((bf16[16,192,128]{2,1,0:T(8,128)(2,1)}), bf16[16,192,128]{2,1,0:T(8,128)(2,1)S(1)}, u32[]{:S(2)}, u32[]{:S(2)}) async-start(bf16[16,192,128]{2,1,0:T(8,128)(2,1)} %tie.9), calls=%async_computation.3 | async-start | bytes 1572864 | tf_op jit(solution)/shard_map/all_to_all | solution.py:354
  116.6 2.0 %collective-permute-start.12 = (bf16[4,1,96,512]{3,2,1,0:T(8,128)(2,1)}, bf16[4,1,96,512]{3,2,1,0:T(8,128)(2,1)S(1)}, u32[]{:S(2)}, u32[]{:S(2)}) collective-permute-start(bf16[4,1,96,512]{3,2,1,0:T(8,128)(2,1)} %collective-permute-done.6.refs_5_.refs_6_), channel_id=1, source_target_pairs={{0,2},{2,0},{4,6},{6,4},{8,10},{10,8},{12,14},{14,12},{16,18},{18,... | collective-permute-start | bytes 1179656 | tf_op jit(solution)/shard_map/ppermute | solution.py:229
  117.0 2.1 %collective-permute-start.14 = (bf16[4,1,96,512]{3,2,1,0:T(8,128)(2,1)}, bf16[4,1,96,512]{3,2,1,0:T(8,128)(2,1)S(1)}, u32[]{:S(2)}, u32[]{:S(2)}) collective-permute-start(bf16[4,1,96,512]{3,2,1,0:T(8,128)(2,1)} %collective-permute-done.8.refs_7_.refs_4_.refs_8_), channel_id=1, source_target_pairs={{0,2},{2,0},{4,6},{6,4},{8,10},{10,8},{12,14},{14,12},{16,18},{18,... | collective-permute-start | bytes 1179656 | tf_op jit(solution)/shard_map/ppermute | solution.py:229
  117.2 2.6 %collective-permute-start.13 = (bf16[4,1,96,512]{3,2,1,0:T(8,128)(2,1)}, bf16[4,1,96,512]{3,2,1,0:T(8,128)(2,1)S(1)}, u32[]{:S(2)}, u32[]{:S(2)}) collective-permute-start(bf16[4,1,96,512]{3,2,1,0:T(8,128)(2,1)} %collective-permute-done.7.refs_6_.refs_3_.refs_7_), channel_id=1, source_target_pairs={{0,2},{2,0},{4,6},{6,4},{8,10},{10,8},{12,14},{14,12},{16,18},{18,... | collective-permute-start | bytes 1179656 | tf_op jit(solution)/shard_map/ppermute | solution.py:229
  118.6 1.1 copy-start.17
  119.2 0.8 copy-start.18
  119.7 0.7 copy-start.19
  136.1 0.9 copy-start.7
